TPU v7x, 32 devices: a whole 2x2x4 slice. The times are simulated.
32 devices in a mesh: blk: 8 (over y, x, core), rep: 4 (over z).
Axes of the slice: x: 2, y: 2, z: 4, core: 2. Of those that a mesh axis runs over, the one named last changes fastest.
Arguments:
- queries: bfloat16 [8192, 4096], P(('blk', 'rep')), as said below
- query_group: int32 [8192, 1], P(('blk', 'rep')), may hold values from 0 to 3; in each aligned block of 256 rows (0 to 255, 256 to 511, ...) at most 128 rows name the same one
- query_bin: int32 [8192], P(('blk', 'rep')), may hold values from 0 to 63
- query_shift: int32 [8192], P(('blk', 'rep')), may hold values from 1 to 2
- library: bfloat16 [4, 256, 4096], P('rep', 'blk'), as said below
- library_bin: int32 [4, 256], P('rep', 'blk'), may hold values from 0 to 63
Outputs:
- best_scores: float32 [8192, 8], P(('blk', 'rep'))
Inputs may be any that keep to these rules, and one draw needn't show every extreme that they name: `query_group`: among the 256 queries of one device at most 128 name the same group, and on every draw some device has a group named by exactly 128 of its queries. `queries`: intensities are nonnegative and every spectrum has peaks. `library`: intensities are nonnegative and every spectrum has peaks.
All inputs are finite; a program needn't handle non-finite values.
Results may differ from a plain program's by a relative error of at most 0.0021.
Values may be sent and summed in bfloat16 or wider, within the bound.
A program may use at most 192 MiB of HBM per device.

v0:
```python
import jax
import jax.numpy as jnp
from jax import lax
from jax.sharding import PartitionSpec as P

W = 4096
K = 8
NSHIFT = 2
SHIFT_BINS = 16
WIN = 16
CAP = 128


def unit_rows(raw):
    values = jnp.sqrt(raw.astype(jnp.float32))
    total = jnp.sum(values * values, axis=-1, keepdims=True)
    return (values * lax.rsqrt(total + 1e-06)).astype(jnp.bfloat16)


def raise_bins(rows, amount):
    head = jnp.zeros(rows.shape[:-1] + (amount,), rows.dtype)
    return jnp.concatenate([head, rows[..., :-amount]], axis=-1)


def slot_index(group, groups, capacity):
    labels = jnp.arange(groups, dtype=jnp.int32)
    onehot = (group[:, None] == labels[None, :]).astype(jnp.int32)
    before = jnp.cumsum(onehot, axis=0) - onehot
    place = jnp.sum(before * onehot, axis=1)
    return group * capacity + place


def stop_scores(plain, shifted, query_bins, lib_bins):
    near = jnp.abs(lib_bins[:, None] - query_bins[None, :]) <= WIN
    return jnp.where(near, jnp.maximum(plain, shifted), 0.0)


def keep_best(best, scores):
    joined = jnp.concatenate([best, scores], axis=0)
    height = joined.shape[0]
    position = lax.broadcasted_iota(jnp.int32, joined.shape, 0)
    picked = []
    for step in range(K):
        top = jnp.max(joined, axis=0)
        first = jnp.min(jnp.where(joined == top[None, :], position, height), axis=0)
        picked.append(top)
        joined = jnp.where(position == first[None, :], -3e38, joined)
    return jnp.stack(picked, axis=0)


def on_device(queries, query_group, query_bin, query_shift, library, library_bin):
    groups = lax.axis_size("rep")
    lib_rows = library.shape[1]
    slots = groups * CAP
    unit_q = unit_rows(queries)
    group = query_group[:, 0]
    slot = slot_index(group, groups, CAP)
    slot_ids = jnp.arange(slots, dtype=jnp.int32)
    placed = slot[:, None] == slot_ids[None, :]
    placed_bf = placed.astype(jnp.bfloat16)
    placed_int = placed.astype(jnp.int32)
    send_q = lax.dot_general(
        placed_bf, unit_q, (((0,), (0,)), ((), ())), preferred_element_type=jnp.float32
    )
    send_q = send_q.astype(jnp.bfloat16).reshape(groups, CAP, W)
    send_bin = jnp.sum(placed_int * query_bin[:, None], axis=0).reshape(groups, CAP)
    send_shift = jnp.sum(placed_int * query_shift[:, None], axis=0).reshape(groups, CAP)
    unit_lib = unit_rows(library)
    bin_row = jnp.pad(library_bin.astype(jnp.bfloat16), ((0, 0), (0, W - lib_rows)))[:, None, :]
    forms = [unit_lib] + [raise_bins(unit_lib, s * SHIFT_BINS) for s in range(1, NSHIFT + 1)]
    stacked_lib = jnp.stack(forms, axis=2)
    bin_forms = jnp.broadcast_to(bin_row[:, :, None, :], (1, 1, NSHIFT + 1, W))
    packed_lib = jnp.concatenate([stacked_lib, bin_forms], axis=1)
    rows = lax.all_to_all(send_q, "rep", split_axis=0, concat_axis=0, tiled=True)
    rbin = lax.all_to_all(send_bin, "rep", split_axis=0, concat_axis=0, tiled=True)
    rshift = lax.all_to_all(send_shift, "rep", split_axis=0, concat_axis=0, tiled=True)
    items = rows.shape[1]
    flat = rows.reshape(-1, W)
    flat_bin = rbin.reshape(-1)
    flat_shift = rshift.reshape(-1)
    total = flat.shape[0]
    start_best = jnp.full((K, total), -1.0, jnp.float32)
    split = lax.all_gather(packed_lib, "blk", axis=1, tiled=True).reshape(
        -1, lib_rows + 1, NSHIFT + 1, W
    )
    blocks = split[:, :lib_rows]
    lib_bins = split[:, lib_rows, 0, :lib_rows].reshape(-1).astype(jnp.int32)
    width = blocks.shape[0] * lib_rows
    forms_flat = blocks.reshape(width * (NSHIFT + 1), W)
    prod = lax.dot_general(
        forms_flat, flat, (((1,), (1,)), ((), ())), preferred_element_type=jnp.float32
    )
    prod = prod.reshape(width, NSHIFT + 1, total)
    shifted = jnp.zeros((width, total), jnp.float32)
    for s in range(1, NSHIFT + 1):
        shifted = jnp.where((flat_shift == s)[None, :], prod[:, s], shifted)
    best = keep_best(start_best, stop_scores(prod[:, 0], shifted, flat_bin, lib_bins))
    results = best.reshape(K, groups, items).transpose(1, 2, 0)
    home = lax.all_to_all(results, "rep", split_axis=0, concat_axis=0, tiled=True)
    back = placed.astype(jnp.float32)
    return jnp.dot(
        back,
        home.reshape(slots, K),
        preferred_element_type=jnp.float32,
        precision=lax.Precision.HIGHEST,
    )


def solution(mesh):
    in_specs = (
        P(("blk", "rep"), None),
        P(("blk", "rep"), None),
        P(("blk", "rep")),
        P(("blk", "rep")),
        P("rep", "blk", None),
        P("rep", "blk"),
    )
    out_specs = P(("blk", "rep"), None)
    return jax.shard_map(
        on_device, mesh=mesh, in_specs=in_specs, out_specs=out_specs, check_vma=False
    )
```

profile of v0, /device:TPU:0, one launch (start us, length us, event | category | flops | bytes accessed | tf_op | source)
XLA Modules:
  0.0 157.6 jit_solution(9246131114150837805)
XLA Ops:
  6.6 1.4 multiply_reduce_fusion.1
  8.0 1.1 multiply_convert_fusion.2
  9.1 1.1 fusion.29
  10.2 0.7 convert_element_type.44
  10.9 0.2 pad_bitcast_fusion
  11.3 1.8 %copy.22 = bf16[1,33,3,4096]{3,2,0,1:T(4,128)(2,1)} copy(bf16[1,33,3,4096]{3,1,2,0:T(8,128)(2,1)S(1)} %pad_maximum_fusion) | data formatting | bytes 1622016 | tf_op jit(solution)/shard_map/concatenate | solution.py:73
  13.1 1.2 reduce-window.6
  14.8 0.8 select_reduce_fusion.8
  15.5 6.3 %all-to-all-start.2 = ((s32[4,1,128]{2,1,0:T(1,128)}), s32[4,1,128]{2,1,0:T(1,128)S(1)}, u32[]{:S(2)}, u32[]{:S(2)}) async-start(s32[4,1,128]{2,1,0:T(1,128)} %bitcast.17), calls=%async_computation.2 | async-start | bytes 4096 | tf_op jit(solution)/shard_map/all_to_all | solution.py:76
  21.8 1.4 multiply_reduce_fusion
  23.3 4.0 %convolution_convert_fusion = bf16[512,4096]{1,0:T(8,128)(2,1)} fusion(bf16[256,4096]{1,0:T(8,128)(2,1)S(1)} %copy-done, f32[256]{0:T(256)S(1)} %add_rsqrt_fusion, s32[256]{0:T(256)S(1)} %bitcast.95), kind=kOutput, calls=%fused_computation | convolution fusion | flops 1079115776 | bytes 6293504 | tf_op jit(solution)/shard_map/dot_general | solution.py:62
  27.3 5.1 %all-to-all-start.1 = ((bf16[4,128,4096]{2,1,0:T(8,128)(2,1)}), bf16[4,128,4096]{2,1,0:T(8,128)(2,1)}, u32[]{:S(2)}, u32[]{:S(2)}) async-start(bf16[4,128,4096]{2,1,0:T(8,128)(2,1)} %bitcast.80), calls=%async_computation.1 | async-start | bytes 8388608 | tf_op jit(solution)/shard_map/all_to_all | solution.py:74
  32.4 39.0 %all-gather.2.cloned.1.call-done = bf16[1,264,3,4096]{3,2,0,1:T(4,128)(2,1)} async-done(((bf16[1,33,3,4096]{3,2,0,1:T(4,128)(2,1)}), bf16[1,264,3,4096]{3,2,0,1:T(4,128)(2,1)}) %all-gather.2.cloned.1.call-update) | async-done | bytes 6488080 | tf_op jit(solution)/shard_map/all_gather | solution.py:83
  71.4 5.6 %slice.40 = bf16[8,32,3,4096]{3,2,1,0:T(4,128)(2,1)S(1)} slice(bf16[8,33,3,4096]{3,2,1,0:T(4,128)(2,1)} %bitcast.81), slice={[0:8], [0:32], [0:3], [0:4096]} | slice | bytes 12582912 | tf_op jit(solution)/shard_map/slice | solution.py:86
  77.0 7.2 %copy.26 = bf16[8,32,3,4096]{3,1,0,2:T(8,128)(2,1)} copy(bf16[8,32,3,4096]{3,2,1,0:T(4,128)(2,1)S(1)} %slice.40) | data formatting | bytes 12582912
  84.2 41.1 %all-to-all-done.1 = bf16[4,128,4096]{2,1,0:T(8,128)(2,1)} async-done(((bf16[4,128,4096]{2,1,0:T(8,128)(2,1)}), bf16[4,128,4096]{2,1,0:T(8,128)(2,1)}, u32[]{:S(2)}, u32[]{:S(2)}) %all-to-all-start.1) | async-done | bytes 4194336 | tf_op jit(solution)/shard_map/all_to_all | solution.py:74
  125.3 3.4 %all-to-all-start = ((s32[4,1,128]{2,1,0:T(1,128)}), s32[4,1,128]{2,1,0:T(1,128)S(1)}, u32[]{:S(2)}, u32[]{:S(2)}) async-start(s32[4,1,128]{2,1,0:T(1,128)} %bitcast.10), calls=%async_computation | async-start | bytes 4096 | tf_op jit(solution)/shard_map/all_to_all | solution.py:75
  128.8 6.8 %fusion.26 = f32[256,3,512]{2,0,1:T(8,128)S(1)} fusion(bf16[256,3,4096]{2,0,1:T(8,128)(2,1)} %bitcast.83, bf16[512,4096,1]{1,0,2:T(8,128)(2,1)} %bitcast.15), kind=kOutput, calls=%fused_computation.70 | convolution fusion | flops 3221225472 | bytes 12058624 | tf_op jit(solution)/shard_map/dot_general | solution.py:90
  135.6 0.7 fusion.24
  136.4 0.2 fusion.10
  137.2 0.2 select_reduce_fusion.5
  137.3 0.1 fusion.25
  137.5 0.2 select_reduce_fusion.4
  137.7 0.2 fusion.13
  137.8 0.2 select_reduce_fusion.3
  138.1 0.2 fusion.18
  138.3 0.3 select_reduce_fusion.2
  138.6 0.3 fusion.12
  138.8 0.3 select_reduce_fusion.1
  139.1 0.3 select_reduce_fusion
  139.5 10.3 %all_to_all.28 = f32[4,128,8]{1,2,0:T(8,128)S(1)} all-to-all(f32[4,128,8]{1,2,0:T(8,128)S(1)} %bitcast.86), channel_id=1, replica_groups=mesh['blk'=8,'rep'=4] {'rep'}, dimensions={0} | all-to-all | bytes 32768 | tf_op jit(solution)/shard_map/all_to_all | solution.py:99
  149.7 1.0 fusion.11
  (34 shorter events, 1.4 us)
Async XLA Ops:
  6.5 6.5 %copy-start.1 = (s32[256,1]{0,1:T(1,128)S(1)}, s32[256,1]{0,1:T(1,128)}, u32[]{:S(2)}) copy-start(s32[256,1]{0,1:T(1,128)} %param.7) | copy-start | bytes 3076
  6.5 8.2 %copy-start.2 = (s32[256]{0:T(256)S(1)}, s32[256]{0:T(256)}, u32[]{:S(2)}) copy-start(s32[256]{0:T(256)} %param.9) | copy-start | bytes 3076
  6.5 8.2 %copy-start.3 = (s32[256]{0:T(256)S(1)}, s32[256]{0:T(256)}, u32[]{:S(2)}) copy-start(s32[256]{0:T(256)} %param.8) | copy-start | bytes 3076
  6.5 15.3 %copy-start = (bf16[256,4096]{1,0:T(8,128)(2,1)S(1)}, bf16[256,4096]{1,0:T(8,128)(2,1)}, u32[]{:S(2)}) copy-start(bf16[256,4096]{1,0:T(8,128)(2,1)} %param.6) | copy-start | bytes 6291460
  6.5 64.9 %all-gather.2.cloned.1.call-start = ((), (), s32[]{:S(2)}) async-start(), calls=%async_computation.4 | async-start | bytes 9732096 | tf_op jit(solution)/shard_map/all_gather | solution.py:83
  15.5 11.8 %all-to-all-start.2 = ((s32[4,1,128]{2,1,0:T(1,128)}), s32[4,1,128]{2,1,0:T(1,128)S(1)}, u32[]{:S(2)}, u32[]{:S(2)}) async-start(s32[4,1,128]{2,1,0:T(1,128)} %bitcast.17), calls=%async_computation.2 | async-start | bytes 4096 | tf_op jit(solution)/shard_map/all_to_all | solution.py:76
  27.3 98.0 %all-to-all-start.1 = ((bf16[4,128,4096]{2,1,0:T(8,128)(2,1)}), bf16[4,128,4096]{2,1,0:T(8,128)(2,1)}, u32[]{:S(2)}, u32[]{:S(2)}) async-start(bf16[4,128,4096]{2,1,0:T(8,128)(2,1)} %bitcast.80), calls=%async_computation.1 | async-start | bytes 8388608 | tf_op jit(solution)/shard_map/all_to_all | solution.py:74
  125.3 11.1 %all-to-all-start = ((s32[4,1,128]{2,1,0:T(1,128)}), s32[4,1,128]{2,1,0:T(1,128)S(1)}, u32[]{:S(2)}, u32[]{:S(2)}) async-start(s32[4,1,128]{2,1,0:T(1,128)} %bitcast.10), calls=%async_computation | async-start | bytes 4096 | tf_op jit(solution)/shard_map/all_to_all | solution.py:75
Sparse Core Ops, SparseCore 0:
  13.2 58.1 all-gather.1
where the time goes:
time: 158 us
  waiting for transfers between devices  80.2 us (51%)
  local copies, waits for them, and re-layouts  15.3 us (10%)
  starting transfers between devices  14.8 us (9%)
  between operations  13.5 us (9%)
  matrix products  11.8 us (7%)
  other arithmetic  11.7 us (7%)
  blocking collectives  10.3 us (7%)
    all_to_all x1, waiting for transfers between devices, on_device(): lax.all_to_all(send_q, 'rep', split_axis=0, concat_axis=0, tiled=True)  41.1 us
    all_gather x1, waiting for transfers between devices, on_device(): lax.all_gather(packed_lib, 'blk', axis=1, tiled=True)  39 us
    all_to_all x1, blocking collectives, on_device(): lax.all_to_all(results, 'rep', split_axis=0, concat_axis=0, tiled=True)  10.3 us
    unnamed x9, local copies, waits for them, and re-layouts  7.24 us
    dot_general x1, matrix products, on_device(): lax.dot_general(forms_flat, flat, (((1,), (1,)), ((), ())), preferred_ele...  6.84 us
    all_to_all x1, starting transfers between devices, on_device(): lax.all_to_all(send_shift, 'rep', split_axis=0, concat_axis=0, tiled=True)  6.32 us
    slice x1, local copies, waits for them, and re-layouts, on_device(): blocks = split[:, :lib_rows]  5.59 us
    all_to_all x1, starting transfers between devices, on_device(): lax.all_to_all(send_q, 'rep', split_axis=0, concat_axis=0, tiled=True)  5.06 us
  transfers between devices with their start and end apart: 4, of which 2 were waited for; matrix products, arithmetic and copies ran while one was open for 18% of the time, Pallas kernels for 0%

commit v1 on v0

v1 whole, which is shorter than its diff:
```python
import functools

import jax
import jax.numpy as jnp
from jax import lax
from jax.experimental import pallas as pl
from jax.experimental.pallas import tpu as pltpu
from jax.sharding import PartitionSpec as P

W = 4096
K = 8
NSHIFT = 2
SHIFT_BINS = 16
WIN = 16
LANES = 128
MESH = pl.DeviceIdType.MESH


def unit_rows(raw):
    values = jnp.sqrt(raw.astype(jnp.float32))
    total = jnp.sum(values * values, axis=-1, keepdims=True)
    return (values * lax.rsqrt(total + 1e-06)).astype(jnp.bfloat16)


def lower_bins(rows, amount):
    tail = jnp.zeros(rows.shape[:-1] + (amount,), rows.dtype)
    return jnp.concatenate([rows[..., amount:], tail], axis=-1)


def general(queries, query_group, query_bin, query_shift, library, library_bin):
    unit_q = unit_rows(queries)
    moved = jnp.zeros_like(unit_q)
    for s in range(1, NSHIFT + 1):
        moved = jnp.where((query_shift == s)[:, None], lower_bins(unit_q, s * SHIFT_BINS), moved)
    both = jnp.concatenate([unit_q, moved], axis=0)
    lib = lax.all_gather(unit_rows(library), "blk", axis=1, tiled=True)
    lib = lax.all_gather(lib, "rep", axis=0, tiled=True)
    bins = lax.all_gather(library_bin, "blk", axis=1, tiled=True)
    bins = lax.all_gather(bins, "rep", axis=0, tiled=True)
    n_q = queries.shape[0]
    score = jnp.zeros((n_q, lib.shape[1]), jnp.float32)
    for g in range(lib.shape[0]):
        prod = lax.dot_general(
            both, lib[g], (((1,), (1,)), ((), ())), preferred_element_type=jnp.float32
        )
        near = jnp.abs(query_bin[:, None] - bins[g][None, :]) <= WIN
        high = jnp.where(near, jnp.maximum(prod[:n_q], prod[n_q:]), 0.0)
        score = jnp.where(query_group == g, high, score)
    position = lax.broadcasted_iota(jnp.int32, score.shape, 1)
    picked = []
    for _ in range(K):
        top = jnp.max(score, axis=1, keepdims=True)
        first = jnp.min(jnp.where(score == top, position, score.shape[1]), axis=1, keepdims=True)
        picked.append(top)
        score = jnp.where(position == first, -3e38, score)
    return jnp.concatenate(picked, axis=1)


def fast_kernel(
    n_rep, rows, q_hbm, lib_ref, libbin_ref, grp_ref, bin_ref, shift_ref, out_ref,
    lib, qraw, qval, qt, best, q_sem,
    zs, zr, xs, xr, ys, yr, xds, xdr, yds, ydr, ss, sr,
):
    b = lax.axis_index("blk")
    z = lax.axis_index("rep")
    core = b % 2
    bx = (b // 2) % 2
    by = b // 4
    sib = b + 1 - 2 * core
    xn = b + 2 - 4 * bx
    yn = b + 4 - 8 * by
    dn = xn + 4 - 8 * by
    half = rows // 2

    qcopy = pltpu.make_async_copy(q_hbm, qraw, q_sem)
    qcopy.start()

    barrier = pltpu.get_barrier_semaphore()
    for other in (sib, xn, yn):
        pl.semaphore_signal(barrier, inc=1, device_id=(other, z), device_id_type=MESH)

    @pl.when(z > 0)
    def _():
        pl.semaphore_signal(barrier, inc=1, device_id=(b, z - 1), device_id_type=MESH)

    @pl.when(z < n_rep - 1)
    def _():
        pl.semaphore_signal(barrier, inc=1, device_id=(b, z + 1), device_id_type=MESH)

    vals = jnp.sqrt(lib_ref[0].astype(jnp.float32))
    total = jnp.sum(vals * vals, axis=-1, keepdims=True)
    mine = pl.ds(pl.multiple_of(b * rows, rows), rows)
    lib[z, mine, 0:W] = (vals * lax.rsqrt(total + 1e-06)).astype(jnp.bfloat16)
    r_id = lax.broadcasted_iota(jnp.int32, (rows, rows), 0)
    c_id = lax.broadcasted_iota(jnp.int32, (rows, rows), 1)
    spread = jnp.where(r_id == c_id, libbin_ref[...].astype(jnp.float32), 0.0)
    column = jnp.sum(spread, axis=1, keepdims=True)
    lib[z, mine, W : W + LANES] = jnp.broadcast_to(column, (rows, LANES)).astype(jnp.bfloat16)

    ends = jnp.where(z == 0, 1, 0) + jnp.where(z == n_rep - 1, 1, 0)
    pl.semaphore_wait(barrier, 5 - ends)

    def order(j):
        m = z // (n_rep // 2)
        zz = z + m * (n_rep - 1 - 2 * z)
        o = jnp.where(j == 0, zz, jnp.where(j == 1, 1 - zz, j))
        return o + m * (n_rep - 1 - 2 * o)

    def shard(p, blk):
        return lib.at[p, pl.ds(pl.multiple_of(blk * rows, rows), rows)]

    def part(p, blk, h):
        return lib.at[p, pl.ds(pl.multiple_of(blk * rows + h * half, half), half)]

    def copy(ref, send, recv, dev):
        return pltpu.make_async_remote_copy(
            src_ref=ref, dst_ref=ref, send_sem=send, recv_sem=recv,
            device_id=dev, device_id_type=MESH,
        )

    def z_up(p):
        return copy(shard(p, b), zs.at[0, p], zr.at[p], (b, z + 1))

    def z_down(p):
        return copy(shard(p, b), zs.at[1, p], zr.at[p], (b, z - 1))

    def x_own(p, blk):
        return copy(shard(p, blk), xs.at[p], xr.at[p], (xn, z))

    def y_own(p, blk):
        return copy(shard(p, blk), ys.at[p], yr.at[p], (yn, z))

    def x_diag(p, blk):
        return copy(part(p, blk, 1), xds.at[p], xdr.at[p], (xn, z))

    def y_diag(p, blk):
        return copy(part(p, blk, 0), yds.at[p], ydr.at[p], (yn, z))

    def to_sib(p, blk, slot):
        return copy(shard(p, blk), ss.at[p, slot], sr.at[p, slot], (sib, z))

    def away(p, do):
        @pl.when((p <= z) & (z < n_rep - 1))
        def _():
            do(z_up(p))

        @pl.when((p >= z) & (z > 0))
        def _():
            do(z_down(p))

    def begin(c):
        c.start()

    def spread_own(p):
        away(p, begin)
        x_own(p, b).start()
        y_own(p, b).start()
        to_sib(p, b, 0).start()

    spread_own(z)

    qcopy.wait()
    step = 512

    def load(i, acc):
        cols = pl.ds(pl.multiple_of(i * step, step), step)
        v = jnp.sqrt(qraw[:, cols].astype(jnp.float32).T)
        qval[cols, :] = v
        return acc + jnp.sum(v * v, axis=0, keepdims=True)

    n_q = qraw.shape[0]
    q_total = lax.fori_loop(0, W // step, load, jnp.zeros((1, n_q), jnp.float32))
    scale = lax.rsqrt(q_total + 1e-06)

    def norm(i, c):
        at = pl.ds(pl.multiple_of(i * step, step), step)
        qt[at, 0:n_q] = (qval[at, :] * scale).astype(jnp.bfloat16)
        return c

    lax.fori_loop(0, W // step, norm, 0)
    qt[pl.ds(W, 2 * SHIFT_BINS), 0:n_q] = jnp.zeros((2 * SHIFT_BINS, n_q), jnp.bfloat16)
    one = shift_ref[...] == 1

    def move(i, c):
        base = pl.multiple_of(i * step, step)
        near = qt[pl.ds(base + SHIFT_BINS, step), 0:n_q].astype(jnp.float32)
        far = qt[pl.ds(base + 2 * SHIFT_BINS, step), 0:n_q].astype(jnp.float32)
        qt[pl.ds(base, step), n_q : 2 * n_q] = jnp.where(one, near, far).astype(jnp.bfloat16)
        return c

    lax.fori_loop(0, W // step, move, 0)
    best[...] = jnp.zeros_like(best)

    def compute(p):
        for slot, blk in enumerate((b, xn, yn, dn)):
            to_sib(p, blk, slot).wait_recv()
        prod = jnp.dot(lib[p, :, 0:W], qt[0:W, :], preferred_element_type=jnp.float32)
        high = jnp.maximum(prod[:, 0:n_q], prod[:, n_q : 2 * n_q])
        bins = lib[p, :, W : W + LANES].astype(jnp.float32)
        bins = jnp.concatenate([bins] * (n_q // LANES), axis=1)
        near = jnp.abs(bins - bin_ref[...].astype(jnp.float32)) <= float(WIN)
        score = jnp.where(near, high, 0.0)
        best[...] = jnp.where(grp_ref[...] == p, score, best[...])

    def stage(t, c):
        @pl.when(t < n_rep)
        def _():
            p = order(t)
            z_up(p).wait_recv()
            spread_own(p)

        @pl.when(t <= n_rep)
        def _():
            p = order(t - 1)
            x_own(p, b).wait_recv()
            y_diag(p, xn).start()
            to_sib(p, xn, 1).start()
            y_own(p, b).wait_recv()
            x_diag(p, yn).start()
            to_sib(p, yn, 2).start()

        @pl.when((t >= 2) & (t <= n_rep + 1))
        def _():
            p = order(t - 2)
            x_diag(p, dn).wait_recv()
            y_diag(p, dn).wait_recv()
            to_sib(p, dn, 3).start()

        @pl.when(t >= 3)
        def _():
            compute(order(t - 3))

        return c

    lax.fori_loop(1, n_rep + 3, stage, 0)

    position = lax.broadcasted_iota(jnp.int32, (K, n_q), 0)
    result = jnp.zeros((K, n_q), jnp.float32)
    filled = jnp.zeros((1, n_q), jnp.int32)
    for _ in range(K):
        cur = best[...]
        top = jnp.max(cur, axis=0, keepdims=True)
        same = cur == top
        count = jnp.sum(same.astype(jnp.int32), axis=0, keepdims=True)
        best[...] = jnp.where(same, -3e38, cur)
        result = jnp.where(position >= filled, top, result)
        filled = filled + count
    out_ref[...] = result

    def finish(p, c):
        away(p, lambda d: d.wait_send())
        x_own(p, b).wait_send()
        y_own(p, b).wait_send()
        y_diag(p, xn).wait_send()
        x_diag(p, yn).wait_send()
        for slot, blk in enumerate((b, xn, yn, dn)):
            to_sib(p, blk, slot).wait_send()
        return c

    lax.fori_loop(0, n_rep, finish, 0)


def fast(n_rep, queries, query_group, query_bin, query_shift, library, library_bin):
    n_q = queries.shape[0]
    rows = library.shape[1]
    lib_g = 8 * rows
    dma = pltpu.SemaphoreType.DMA
    vmem = pl.BlockSpec(memory_space=pltpu.VMEM)
    top = pl.pallas_call(
        functools.partial(fast_kernel, n_rep, rows),
        out_shape=jax.ShapeDtypeStruct((K, n_q), jnp.float32),
        in_specs=[pl.BlockSpec(memory_space=pl.ANY)] + [vmem] * 5,
        out_specs=vmem,
        scratch_shapes=[
            pltpu.VMEM((n_rep, lib_g, W + LANES), jnp.bfloat16),
            pltpu.VMEM((n_q, W), jnp.bfloat16),
            pltpu.VMEM((W, n_q), jnp.float32),
            pltpu.VMEM((W + 2 * SHIFT_BINS, 2 * n_q), jnp.bfloat16),
            pltpu.VMEM((lib_g, n_q), jnp.float32),
            dma(()),
            dma((2, n_rep)), dma((n_rep,)),
            dma((n_rep,)), dma((n_rep,)), dma((n_rep,)), dma((n_rep,)),
            dma((n_rep,)), dma((n_rep,)), dma((n_rep,)), dma((n_rep,)),
            dma((n_rep, 4)), dma((n_rep, 4)),
        ],
        compiler_params=pltpu.CompilerParams(
            collective_id=0, has_side_effects=True, vmem_limit_bytes=48 * 1024 * 1024
        ),
    )(
        queries,
        library,
        library_bin,
        query_group.reshape(1, n_q),
        query_bin.reshape(1, n_q),
        query_shift.reshape(1, n_q),
    )
    return top.T


def solution(mesh):
    in_specs = (
        P(("blk", "rep"), None),
        P(("blk", "rep"), None),
        P(("blk", "rep")),
        P(("blk", "rep")),
        P("rep", "blk", None),
        P("rep", "blk"),
    )
    out_specs = P(("blk", "rep"), None)
    if mesh.shape["blk"] == 8 and mesh.shape["rep"] == 4:
        body = functools.partial(fast, mesh.shape["rep"])
    else:
        body = general
    return jax.shard_map(
        body, mesh=mesh, in_specs=in_specs, out_specs=out_specs, check_vma=False
    )
```

time: 158 us -> 51.6 us (0.33)
  waiting for transfers between devices: 80.2 us -> 0 us
  Pallas kernels: 0 us -> 45.6 us
  starting transfers between devices: 14.8 us -> 0 us
  between operations: 13.5 us -> 0.02 us
  matrix products: 11.8 us -> 0 us
  other arithmetic: 11.7 us -> 0 us
  blocking collectives: 10.3 us -> 0 us
  local copies, waits for them, and re-layouts: 15.3 us -> 5.83 us
    pallas_call x0 -> x1, Pallas kernels: none -> 45.6 us  [fast(): pl.pallas_call(functools.partial(fast_kernel, n_rep, rows), out_shape=jax...]
    all_to_all x3 -> x0, waiting for transfers between devices: 41.1 us -> none  [the longest x1 41.1 us: on_device(): lax.all_to_all(send_q, 'rep', split_axis=0, concat_axis=0, tiled=True)]
    all_gather x1 -> x0, waiting for transfers between devices: 39 us -> none  [on_device(): lax.all_gather(packed_lib, 'blk', axis=1, tiled=True)]
    all_to_all x3 -> x0, starting transfers between devices: 14.8 us -> none  [the longest x1 6.32 us: on_device(): lax.all_to_all(send_shift, 'rep', split_axis=0, concat_axis=0, tiled=True)]
    dot_general x3 -> x0, matrix products: 11.8 us -> none  [the longest x1 6.84 us: on_device(): lax.dot_general(forms_flat, flat, (((1,), (1,)), ((), ())), preferred_ele...]
    all_to_all x1 -> x0, blocking collectives: 10.3 us -> none  [on_device(): lax.all_to_all(results, 'rep', split_axis=0, concat_axis=0, tiled=True)]
    slice x3 -> x0, local copies, waits for them, and re-layouts: 5.77 us -> none  [the longest x1 5.59 us: on_device(): blocks = split[:, :lib_rows]]
    reduce_sum x4 -> x0, other arithmetic: 3.59 us -> none  [the longest x2 2.81 us: unit_rows(): total = jnp.sum(values * values, axis=-1, keepdims=True)]
  transfers between devices with their start and end apart: 4 -> 0, of which waited for: 2 -> 0; matrix products, arithmetic and copies ran while one was open for 18% -> 0% of each run, Pallas kernels for 0% -> 0%
where the time goes in v1:
time: 51.6 us; the launch traced here: 51.4 us
  Pallas kernels  45.6 us (88%)
  local copies, waits for them, and re-layouts  5.83 us (11%)
    pallas_call x1, Pallas kernels, fast(): pl.pallas_call(functools.partial(fast_kernel, n_rep, rows), out_shape=jax...  45.6 us
    unnamed x13, local copies, waits for them, and re-layouts  5.83 us

profile of v1, /device:TPU:0, one launch (start us, length us, event | category | flops | bytes accessed | tf_op | source)
XLA Modules:
  0.0 51.4 jit_solution(4556735130114446885)
XLA Ops:
  0.0 0.0 copy-start
  0.0 1.6 %copy-done = bf16[256,4096]{1,0:T(8,128)(2,1)S(1)} copy-done((bf16[256,4096]{1,0:T(8,128)(2,1)S(1)}, bf16[256,4096]{1,0:T(8,128)(2,1)}, u32[]{:S(2)}) %copy-start) | copy-done | bytes 2097176
  1.6 0.0 copy-start.1
  1.6 0.9 %copy-done.1 = bf16[1,32,4096]{2,1,0:T(8,128)(2,1)S(1)} copy-done((bf16[1,32,4096]{2,1,0:T(8,128)(2,1)S(1)}, bf16[1,32,4096]{2,1,0:T(8,128)(2,1)}, u32[]{:S(2)}) %copy-start.1) | copy-done | bytes 262168
  2.5 0.0 copy-start.2
  2.5 0.7 %copy-done.2 = s32[256,1]{0,1:T(1,128)S(1)} copy-done((s32[256,1]{0,1:T(1,128)S(1)}, s32[256,1]{0,1:T(1,128)}, u32[]{:S(2)}) %copy-start.2) | copy-done | bytes 1048
  3.2 0.0 copy-start.3
  3.2 0.7 %copy-done.3 = s32[256]{0:T(256)S(1)} copy-done((s32[256]{0:T(256)S(1)}, s32[256]{0:T(256)}, u32[]{:S(2)}) %copy-start.3) | copy-done | bytes 1048
  3.9 0.0 copy-start.4
  3.9 0.7 %copy-done.4 = s32[256]{0:T(256)S(1)} copy-done((s32[256]{0:T(256)S(1)}, s32[256]{0:T(256)}, u32[]{:S(2)}) %copy-start.4) | copy-done | bytes 1048
  4.6 0.0 copy-start.5
  4.6 0.7 %copy-done.5 = s32[1,32]{1,0:T(1,128)S(1)} copy-done((s32[1,32]{1,0:T(1,128)S(1)}, s32[1,32]{1,0:T(1,128)}, u32[]{:S(2)}) %copy-start.5) | copy-done | bytes 152
  5.2 45.6 %shard_map.64 = f32[8,256]{1,0:T(8,128)S(1)} custom-call(bf16[256,4096]{1,0:T(8,128)(2,1)S(1)} %copy-done, bf16[1,32,4096]{2,1,0:T(8,128)(2,1)S(1)} %copy-done.1, s32[1,32]{1,0:T(1,128)S(1)} %copy-done.5, s32[1,256]{1,0:T(1,128)S(1)} %bitcast.5, s32[1,256]{1,0:T(1,128)S(1)} %bitcast.6, s32[1,256]{1,0:T(1,128)S(1)} %bitcast.7), custom_call_target="tpu_custom_call" | custom-call | tf_op jit(solution)/shard_map/pallas_call | solution.py:269
  50.8 0.6 %copy.8 = f32[256,8]{0,1:T(8,128)} copy(f32[256,8]{0,1:T(8,128)S(1)} %bitcast.4) | data formatting | bytes 16384
Async XLA Ops:
  0.0 1.6 %copy-start = (bf16[256,4096]{1,0:T(8,128)(2,1)S(1)}, bf16[256,4096]{1,0:T(8,128)(2,1)}, u32[]{:S(2)}) copy-start(bf16[256,4096]{1,0:T(8,128)(2,1)} %q_hbm.1) | copy-start | bytes 6291460
  1.6 0.9 %copy-start.1 = (bf16[1,32,4096]{2,1,0:T(8,128)(2,1)S(1)}, bf16[1,32,4096]{2,1,0:T(8,128)(2,1)}, u32[]{:S(2)}) copy-start(bf16[1,32,4096]{2,1,0:T(8,128)(2,1)} %lib_ref.1) | copy-start | bytes 786436
  2.5 0.7 %copy-start.2 = (s32[256,1]{0,1:T(1,128)S(1)}, s32[256,1]{0,1:T(1,128)}, u32[]{:S(2)}) copy-start(s32[256,1]{0,1:T(1,128)} %param.7) | copy-start | bytes 3076
  3.2 0.7 %copy-start.3 = (s32[256]{0:T(256)S(1)}, s32[256]{0:T(256)}, u32[]{:S(2)}) copy-start(s32[256]{0:T(256)} %param.8) | copy-start | bytes 3076
  3.9 0.7 %copy-start.4 = (s32[256]{0:T(256)S(1)}, s32[256]{0:T(256)}, u32[]{:S(2)}) copy-start(s32[256]{0:T(256)} %param.9) | copy-start | bytes 3076
  4.6 0.7 %copy-start.5 = (s32[1,32]{1,0:T(1,128)S(1)}, s32[1,32]{1,0:T(1,128)}, u32[]{:S(2)}) copy-start(s32[1,32]{1,0:T(1,128)} %libbin_ref.1) | copy-start | bytes 388

commit v2 on v1

--- a/solution.py
+++ b/solution.py
@@ -57,9 +57,9 @@
 
 
 def fast_kernel(
-    n_rep, rows, q_hbm, lib_ref, libbin_ref, grp_ref, bin_ref, shift_ref, out_ref,
-    lib, qraw, qval, qt, best, q_sem,
-    zs, zr, xs, xr, ys, yr, xds, xdr, yds, ydr, ss, sr,
+    n_rep, rows, q_hbm, lib_hbm, libbin_hbm, grp_hbm, bin_hbm, shift_hbm, out_ref,
+    lib, qraw, qval, qt, best, lib_ref, libbin_ref, grp_ref, bin_ref, shift_ref, in_sem,
+    zs, zr, xs, xr, ys, yr, xds, xdr, yds, ydr, ss, sr, zds, zdr, hs, hr,
 ):
     b = lax.axis_index("blk")
     z = lax.axis_index("rep")
@@ -72,8 +72,13 @@
     dn = xn + 4 - 8 * by
     half = rows // 2
 
-    qcopy = pltpu.make_async_copy(q_hbm, qraw, q_sem)
-    qcopy.start()
+    pairs = (
+        (lib_hbm, lib_ref), (libbin_hbm, libbin_ref), (q_hbm, qraw),
+        (grp_hbm, grp_ref), (bin_hbm, bin_ref), (shift_hbm, shift_ref),
+    )
+    loads = [pltpu.make_async_copy(a, d, in_sem.at[i]) for i, (a, d) in enumerate(pairs)]
+    for c in loads:
+        c.start()
 
     barrier = pltpu.get_barrier_semaphore()
     for other in (sib, xn, yn):
@@ -87,6 +92,8 @@
     def _():
         pl.semaphore_signal(barrier, inc=1, device_id=(b, z + 1), device_id_type=MESH)
 
+    loads[0].wait()
+    loads[1].wait()
     vals = jnp.sqrt(lib_ref[0].astype(jnp.float32))
     total = jnp.sum(vals * vals, axis=-1, keepdims=True)
     mine = pl.ds(pl.multiple_of(b * rows, rows), rows)
@@ -94,8 +101,8 @@
     r_id = lax.broadcasted_iota(jnp.int32, (rows, rows), 0)
     c_id = lax.broadcasted_iota(jnp.int32, (rows, rows), 1)
     spread = jnp.where(r_id == c_id, libbin_ref[...].astype(jnp.float32), 0.0)
-    column = jnp.sum(spread, axis=1, keepdims=True)
-    lib[z, mine, W : W + LANES] = jnp.broadcast_to(column, (rows, LANES)).astype(jnp.bfloat16)
+    own_bins = jnp.sum(spread, axis=1, keepdims=True)
+    lib[z, mine, W : W + LANES] = jnp.broadcast_to(own_bins, (rows, LANES)).astype(jnp.bfloat16)
 
     ends = jnp.where(z == 0, 1, 0) + jnp.where(z == n_rep - 1, 1, 0)
     pl.semaphore_wait(barrier, 5 - ends)
@@ -109,8 +116,11 @@
     def shard(p, blk):
         return lib.at[p, pl.ds(pl.multiple_of(blk * rows, rows), rows)]
 
-    def part(p, blk, h):
-        return lib.at[p, pl.ds(pl.multiple_of(blk * rows + h * half, half), half)]
+    split = (W // 2 + LANES, W // 2)
+
+    def part(p, blk, h, c):
+        at = pl.ds(pl.multiple_of(blk * rows + h * half, half), half)
+        return lib.at[p, at, pl.ds(c * split[0], split[c])]
 
     def copy(ref, send, recv, dev):
         return pltpu.make_async_remote_copy(
@@ -131,35 +141,56 @@
         return copy(shard(p, blk), ys.at[p], yr.at[p], (yn, z))
 
     def x_diag(p, blk):
-        return copy(part(p, blk, 1), xds.at[p], xdr.at[p], (xn, z))
+        return copy(part(p, blk, 1, 1), xds.at[p], xdr.at[p], (xn, z))
 
     def y_diag(p, blk):
-        return copy(part(p, blk, 0), yds.at[p], ydr.at[p], (yn, z))
+        return copy(part(p, blk, 1, 0), yds.at[p], ydr.at[p], (yn, z))
+
+    def x_home(blk):
+        return copy(part(z, blk, 0, 1), hs.at[0], hr.at[0], (xn, z))
+
+    def y_home(blk):
+        return copy(part(z, blk, 0, 0), hs.at[1], hr.at[1], (yn, z))
+
+    def top_half(p):
+        return lib.at[p, pl.ds(pl.multiple_of(dn * rows, half), half)]
+
+    def zd_up(p):
+        return copy(top_half(p), zds.at[0, p], zdr.at[p], (b, z + 1))
+
+    def zd_down(p):
+        return copy(top_half(p), zds.at[1, p], zdr.at[p], (b, z - 1))
 
     def to_sib(p, blk, slot):
         return copy(shard(p, blk), ss.at[p, slot], sr.at[p, slot], (sib, z))
 
-    def away(p, do):
+    def away(p, up, down, do):
         @pl.when((p <= z) & (z < n_rep - 1))
         def _():
-            do(z_up(p))
+            do(up(p))
 
         @pl.when((p >= z) & (z > 0))
         def _():
-            do(z_down(p))
+            do(down(p))
 
     def begin(c):
         c.start()
 
     def spread_own(p):
-        away(p, begin)
+        away(p, z_up, z_down, begin)
         x_own(p, b).start()
         y_own(p, b).start()
         to_sib(p, b, 0).start()
 
+    def column(t):
+        p = order(t)
+        z_up(p).wait_recv()
+        spread_own(p)
+
     spread_own(z)
 
-    qcopy.wait()
+    for c in loads[2:]:
+        c.wait()
     step = 512
 
     def load(i, acc):
@@ -171,6 +202,16 @@
     n_q = qraw.shape[0]
     q_total = lax.fori_loop(0, W // step, load, jnp.zeros((1, n_q), jnp.float32))
     scale = lax.rsqrt(q_total + 1e-06)
+
+    x_own(z, b).wait_recv()
+    y_home(xn).start()
+    y_own(z, b).wait_recv()
+    x_home(yn).start()
+    y_diag(z, xn).start()
+    to_sib(z, xn, 1).start()
+    x_diag(z, yn).start()
+    to_sib(z, yn, 2).start()
+    column(1)
 
     def norm(i, c):
         at = pl.ds(pl.multiple_of(i * step, step), step)
@@ -205,9 +246,7 @@
     def stage(t, c):
         @pl.when(t < n_rep)
         def _():
-            p = order(t)
-            z_up(p).wait_recv()
-            spread_own(p)
+            column(t)
 
         @pl.when(t <= n_rep)
         def _():
@@ -219,7 +258,19 @@
             x_diag(p, yn).start()
             to_sib(p, yn, 2).start()
 
-        @pl.when((t >= 2) & (t <= n_rep + 1))
+        @pl.when(t == 2)
+        def _():
+            x_home(dn).wait_recv()
+            y_home(dn).wait_recv()
+            away(z, zd_up, zd_down, begin)
+
+        @pl.when(t <= n_rep)
+        def _():
+            p = order(t - 1)
+            zd_up(p).wait_recv()
+            away(p, zd_up, zd_down, begin)
+
+        @pl.when(t <= n_rep + 1)
         def _():
             p = order(t - 2)
             x_diag(p, dn).wait_recv()
@@ -232,7 +283,7 @@
 
         return c
 
-    lax.fori_loop(1, n_rep + 3, stage, 0)
+    lax.fori_loop(2, n_rep + 3, stage, 0)
 
     position = lax.broadcasted_iota(jnp.int32, (K, n_q), 0)
     result = jnp.zeros((K, n_q), jnp.float32)
@@ -248,7 +299,8 @@
     out_ref[...] = result
 
     def finish(p, c):
-        away(p, lambda d: d.wait_send())
+        away(p, z_up, z_down, lambda d: d.wait_send())
+        away(p, zd_up, zd_down, lambda d: d.wait_send())
         x_own(p, b).wait_send()
         y_own(p, b).wait_send()
         y_diag(p, xn).wait_send()
@@ -258,6 +310,8 @@
         return c
 
     lax.fori_loop(0, n_rep, finish, 0)
+    x_home(yn).wait_send()
+    y_home(xn).wait_send()
 
 
 def fast(n_rep, queries, query_group, query_bin, query_shift, library, library_bin):
@@ -269,7 +323,7 @@
     top = pl.pallas_call(
         functools.partial(fast_kernel, n_rep, rows),
         out_shape=jax.ShapeDtypeStruct((K, n_q), jnp.float32),
-        in_specs=[pl.BlockSpec(memory_space=pl.ANY)] + [vmem] * 5,
+        in_specs=[pl.BlockSpec(memory_space=pltpu.HBM)] * 6,
         out_specs=vmem,
         scratch_shapes=[
             pltpu.VMEM((n_rep, lib_g, W + LANES), jnp.bfloat16),
@@ -277,14 +331,20 @@
             pltpu.VMEM((W, n_q), jnp.float32),
             pltpu.VMEM((W + 2 * SHIFT_BINS, 2 * n_q), jnp.bfloat16),
             pltpu.VMEM((lib_g, n_q), jnp.float32),
-            dma(()),
+            pltpu.VMEM((1, rows, W), jnp.bfloat16),
+            pltpu.VMEM((1, rows), jnp.int32),
+            pltpu.VMEM((1, n_q), jnp.int32),
+            pltpu.VMEM((1, n_q), jnp.int32),
+            pltpu.VMEM((1, n_q), jnp.int32),
+            dma((6,)),
             dma((2, n_rep)), dma((n_rep,)),
             dma((n_rep,)), dma((n_rep,)), dma((n_rep,)), dma((n_rep,)),
             dma((n_rep,)), dma((n_rep,)), dma((n_rep,)), dma((n_rep,)),
             dma((n_rep, 4)), dma((n_rep, 4)),
+            dma((2, n_rep)), dma((n_rep,)), dma((2,)), dma((2,)),
         ],
         compiler_params=pltpu.CompilerParams(
-            collective_id=0, has_side_effects=True, vmem_limit_bytes=48 * 1024 * 1024
+            collective_id=0, has_side_effects=True, vmem_limit_bytes=64 * 1024 * 1024 - 65536
         ),
     )(
         queries,

time: 51.6 us -> 48.3 us (0.936)
  local copies, waits for them, and re-layouts: 5.83 us -> 1.3 us
  Pallas kernels: 45.6 us -> 46.8 us
    unnamed x13 -> x1, local copies, waits for them, and re-layouts: 5.83 us -> 1.3 us
    pallas_call x1, Pallas kernels: 45.6 us -> 46.8 us  [fast(): pl.pallas_call(functools.partial(fast_kernel, n_rep, rows), out_shape=jax...]
where the time goes in v2:
time: 48.3 us; the launch traced here: 48.1 us
  Pallas kernels  46.8 us (97%)
  local copies, waits for them, and re-layouts  1.3 us (3%)
    pallas_call x1, Pallas kernels, fast(): pl.pallas_call(functools.partial(fast_kernel, n_rep, rows), out_shape=jax...  46.8 us
    unnamed x1, local copies, waits for them, and re-layouts  1.3 us

profile of v2, /device:TPU:0, one launch (start us, length us, event | category | flops | bytes accessed | tf_op | source)
XLA Modules:
  0.0 48.1 jit_solution(13401076166340737417)
XLA Ops:
  0.0 46.8 %shard_map.64 = f32[8,256]{1,0:T(8,128)} custom-call(bf16[256,4096]{1,0:T(8,128)(2,1)} %q_hbm.1, bf16[1,32,4096]{2,1,0:T(8,128)(2,1)} %lib_hbm.1, s32[1,32]{1,0:T(1,128)} %libbin_hbm.1, s32[1,256]{1,0:T(1,128)} %bitcast.5, s32[1,256]{1,0:T(1,128)} %bitcast.6, s32[1,256]{1,0:T(1,128)} %bitcast.7), custom_call_target="tpu_custom_call" | custom-call | tf_op jit(solution)/shard_map/pallas_call | solution.py:323
  46.8 1.3 %copy.8 = f32[256,8]{0,1:T(8,128)} copy(f32[256,8]{0,1:T(8,128)} %bitcast.4) | data formatting | bytes 16384
